TPU v7x, 32 devices: a whole 2x2x4 slice. The times are simulated.
32 devices in a mesh: fac: 8 (over z, y), scn: 4 (over x, core).
Axes of the slice: x: 2, y: 2, z: 4, core: 2. Of those that a mesh axis runs over, the one named last changes fastest.
Arguments:
- loadings: bfloat16 [49152, 512], P('fac'), may hold values from -0.25 to 0.25
- draws: bfloat16 [512, 3072], P(None, 'scn'), may hold values from -6 to 6
- delta: float32 [49152], P('fac'), may hold values from -0.02734375 to 0.02734375
- gamma: bfloat16 [128, 128, 128], P('fac', 'scn'), may hold values from -0.0029296875 to 0.0029296875
- pair_rows: int32 [128], replicated, may hold values from 0 to 383, as said below
- pair_cols: int32 [128], replicated, may hold values from 0 to 383, as said below
- pair_count: int32 [8], replicated, may hold values from 4 to 16, as said below
Outputs:
- pnl: float32 [3072], P('scn')
Inputs may be any that keep to these rules, and one draw needn't show every extreme that they name: Block numbers of the slots; for every owner o, among the 32 entries pair_rows and pair_cols of its slots (live or not), the blocks of each index h of fac (blocks h * 48 to h * 48 + 47) are named at most 5 times, and for every owner some index h is named exactly 5 times. `pair_cols`: see pair_rows; the bound holds with both lists together. An owner's live slots are its first pair_count slots; some owner has all 16 slots live.
All inputs are finite; a program needn't handle non-finite values.
Results may differ from a plain program's by a relative error of at most 0.002.
Values may be sent and summed in bfloat16 or wider, within the bound.
A program may use at most 128 MiB of HBM per device.

v0:
```python
import jax
import jax.numpy as jnp
from jax import lax
from jax.sharding import PartitionSpec as P


def on_device(loadings, draws, delta, gamma, pair_rows, pair_cols, pair_count):
    owners = lax.axis_size("fac")
    my_index = lax.axis_index("fac")
    capacity = gamma.shape[0]
    block_rows = gamma.shape[2]
    local_blocks = loadings.shape[0] // block_rows
    factor_draws = loadings.shape[1]
    columns = draws.shape[1]
    per_source = 2 * capacity // owners + 1
    wanted = jnp.stack(
        [pair_rows.reshape(owners, capacity), pair_cols.reshape(owners, capacity)], axis=2
    ).reshape(owners, 2 * capacity)
    source = wanted // local_blocks
    offset = wanted - source * local_blocks
    request_order = jnp.arange(2 * capacity, dtype=jnp.int32)
    same_source = source[:, :, None] == source[:, None, :]
    earlier = request_order[None, :] < request_order[:, None]
    position = jnp.sum((same_source & earlier[None, :, :]).astype(jnp.int32), axis=2)
    slot_index = jnp.arange(per_source, dtype=jnp.int32)
    chosen = (source == my_index)[:, :, None] & (position[:, :, None] == slot_index[None, None, :])
    outgoing = jnp.sum(chosen.astype(jnp.int32) * offset[:, :, None], axis=1).reshape(-1)
    my_source = lax.dynamic_index_in_dim(source, my_index, 0, keepdims=False)
    my_position = lax.dynamic_index_in_dim(position, my_index, 0, keepdims=False)
    arrival = my_source * per_source + my_position
    loading_rows = loadings.reshape(local_blocks, block_rows, factor_draws)
    outbound = loading_rows[outgoing].reshape(owners, per_source, block_rows, factor_draws)
    inbound = lax.all_to_all(outbound, "fac", split_axis=0, concat_axis=0, tiled=True)
    picked = inbound.reshape(owners * per_source, block_rows, factor_draws)[arrival]
    needed = jnp.einsum("rbk,ks->rbs", picked, draws, preferred_element_type=jnp.float32).astype(
        jnp.bfloat16
    )
    folded = jnp.dot(
        delta[None, :],
        loadings,
        preferred_element_type=jnp.float32,
        precision=lax.Precision.HIGHEST,
    )
    linear = jnp.dot(
        folded, draws, preferred_element_type=jnp.float32, precision=lax.Precision.HIGHEST
    )[0]
    paired = needed.reshape(capacity, 2, block_rows, columns)
    left_block = paired[:, 0]
    right_block = paired[:, 1]
    my_wanted = lax.dynamic_index_in_dim(wanted, my_index, 0, keepdims=False).reshape(capacity, 2)
    my_count = lax.dynamic_index_in_dim(pair_count, my_index, 0, keepdims=False)
    is_live = (jnp.arange(capacity, dtype=jnp.int32) < my_count).astype(jnp.float32)
    weight = jnp.where(my_wanted[:, 0] == my_wanted[:, 1], 1.0, 2.0).astype(jnp.float32) * is_live
    product = jnp.einsum(
        "cab,cbs->cas",
        lax.all_gather(gamma, "scn", axis=1, tiled=True),
        right_block,
        preferred_element_type=jnp.float32,
    )
    inner = jnp.sum(product * left_block, axis=1)
    quad = jnp.sum(weight[:, None] * inner, axis=0)
    return lax.psum(linear + 0.5 * quad, "fac")


def solution(mesh):
    in_specs = (P("fac", None), P(None, "scn"), P("fac"), P("fac", "scn", None), P(), P(), P())
    out_specs = P("scn")
    return jax.shard_map(
        on_device, mesh=mesh, in_specs=in_specs, out_specs=out_specs, check_vma=False
    )
```

profile of v0, /device:TPU:0, one launch (start us, length us, event | category | flops | bytes accessed | tf_op | source)
XLA Modules:
  0.0 165.2 jit_solution(6089969389103025652)
XLA Ops:
  0.0 0.0 copy-start
  0.0 0.8 stack_reshape.6
  0.8 0.7 stack_reshape.7
  1.6 0.1 copy.26
  1.6 0.1 copy.27
  1.8 0.3 convert_reduce_fusion
  2.1 0.2 select_reduce_fusion
  2.2 0.1 copy.31
  2.3 0.1 reshape.170
  2.4 7.4 %gather_fusion = bf16[40,128,512]{2,1,0:T(8,128)(2,1)} fusion(bf16[48,128,512]{2,1,0:T(8,128)(2,1)} %bitcast.41, s32[1024]{0:T(1024)S(1)} %pad_clamp_fusion.1), kind=kCustom, calls=%fused_computation | custom fusion | bytes 10485920 | tf_op jit(solution)/shard_map/gather | solution.py:32
  9.9 0.0 copy-start.3
  9.9 0.0 copy-start.2
  9.9 7.4 %all-to-all-start = ((bf16[8,5,128,512]{3,2,1,0:T(8,128)(2,1)}), bf16[8,5,128,512]{3,2,1,0:T(8,128)(2,1)}, u32[]{:S(2)}, u32[]{:S(2)}) async-start(bf16[8,5,128,512]{3,2,1,0:T(8,128)(2,1)} %bitcast.42), calls=%async_computation | async-start | bytes 10485760 | tf_op jit(solution)/shard_map/all_to_all | solution.py:33
  17.3 0.0 copy-start.1
  17.3 0.2 dynamic-slice_reduce_fusion
  17.5 0.1 reshape.168
  17.6 0.0 copy-done.3
  17.6 0.6 dynamic_slice.14
  18.2 0.8 select_reduce_fusion.1
  19.0 0.0 copy-done.2
  19.0 4.5 %convolution_bitcast_fusion = f32[512,1]{0,1:T(1,128)S(1)} fusion(f32[6144,1]{0,1:T(1,128)S(1)} %bitcast.45, bf16[6144,512]{1,0:T(8,128)(2,1)} %param.7), kind=kOutput, calls=%fused_computation.9 | convolution fusion | flops 37748736 | bytes 6318080 | tf_op jit(solution)/shard_map/dot_general | solution.py:38
  23.6 0.0 copy-done
  23.6 0.4 convolution_reduce_fusion
  24.0 0.0 copy-done.1
  24.0 7.2 %all_gather.3 = bf16[16,128,128]{2,1,0:T(8,128)(2,1)S(1)} all-gather(bf16[16,32,128]{2,1,0:T(8,128)(2,1)S(1)} %copy-done.1), channel_id=1, replica_groups=mesh['fac'=8,'scn'=4] {'scn'}, dimensions={1}, use_global_device_ids=true | all-gather | bytes 655360 | tf_op jit(solution)/shard_map/all_gather | solution.py:56
  31.2 101.9 %all-to-all-done = bf16[8,5,128,512]{3,2,1,0:T(8,128)(2,1)} async-done(((bf16[8,5,128,512]{3,2,1,0:T(8,128)(2,1)}), bf16[8,5,128,512]{3,2,1,0:T(8,128)(2,1)}, u32[]{:S(2)}, u32[]{:S(2)}) %all-to-all-start) | async-done | bytes 5242912 | tf_op jit(solution)/shard_map/all_to_all | solution.py:33
  133.1 5.3 %gather_fusion.1 = bf16[32,128,512]{2,1,0:T(8,128)(2,1)} fusion(bf16[40,128,512]{2,1,0:T(8,128)(2,1)} %bitcast.8, s32[1024]{0:T(1024)S(1)} %pad_clamp_fusion), kind=kCustom, calls=%fused_computation.1 | custom fusion | bytes 8388736 | tf_op jit(solution)/shard_map/gather | solution.py:34
  138.4 5.6 %convolution_convert_fusion = bf16[32,128,768]{2,1,0:T(8,128)(2,1)S(1)} fusion(bf16[32,128,512]{2,1,0:T(8,128)(2,1)} %gather_fusion.1, bf16[512,768]{1,0:T(8,128)(2,1)S(1)} %copy-done), kind=kOutput, calls=%fused_computation.4 | convolution fusion | flops 3224371200 | bytes 11272192 | tf_op jit(solution)/shard_map/rbk,ks->rbs/dot_general | solution.py:35
  144.0 1.0 fusion
  145.0 0.1 multiply_reduce_fusion
  145.1 20.1 %psum.7 = f32[768]{0:T(1024)} all-reduce(f32[768]{0:T(1024)S(1)} %multiply_add_fusion), channel_id=1, replica_groups=mesh['fac'=8,'scn'=4] {'fac'}, use_global_device_ids=true, to_apply=%region_4.5 | all-reduce | flops 768 | bytes 6144 | tf_op jit(solution)/shard_map/psum | solution.py:62
  (9 shorter events, 0.1 us)
Async XLA Ops:
  0.0 23.6 %copy-start = (bf16[512,768]{1,0:T(8,128)(2,1)S(1)}, bf16[512,768]{1,0:T(8,128)(2,1)}, u32[]{:S(2)}) copy-start(bf16[512,768]{1,0:T(8,128)(2,1)} %param.8) | copy-start | bytes 2359300
  9.9 7.7 %copy-start.3 = (s32[8]{0:T(128)S(1)}, s32[8]{0:T(128)}, u32[]{:S(2)}) copy-start(s32[8]{0:T(128)} %param.13) | copy-start | bytes 100
  9.9 9.1 %copy-start.2 = (f32[6144]{0:T(1024)S(1)}, f32[6144]{0:T(1024)}, u32[]{:S(2)}) copy-start(f32[6144]{0:T(1024)} %param.9) | copy-start | bytes 73732
  9.9 123.2 %all-to-all-start = ((bf16[8,5,128,512]{3,2,1,0:T(8,128)(2,1)}), bf16[8,5,128,512]{3,2,1,0:T(8,128)(2,1)}, u32[]{:S(2)}, u32[]{:S(2)}) async-start(bf16[8,5,128,512]{3,2,1,0:T(8,128)(2,1)} %bitcast.42), calls=%async_computation | async-start | bytes 10485760 | tf_op jit(solution)/shard_map/all_to_all | solution.py:33
  17.3 6.7 %copy-start.1 = (bf16[16,32,128]{2,1,0:T(8,128)(2,1)S(1)}, bf16[16,32,128]{2,1,0:T(8,128)(2,1)}, u32[]{:S(2)}) copy-start(bf16[16,32,128]{2,1,0:T(8,128)(2,1)} %param.10) | copy-start | bytes 393220
where the time goes:
time: 166 us; the launch traced here: 165 us
  waiting for transfers between devices  102 us (61%)
  blocking collectives  27.2 us (16%)
  local copies, waits for them, and re-layouts  15.5 us (9%)
  matrix products  11.6 us (7%)
  starting transfers between devices  7.41 us (4%)
    all_to_all x1, waiting for transfers between devices, on_device(): lax.all_to_all(outbound, 'fac', split_axis=0, concat_axis=0, tiled=True)  102 us
    psum x1, blocking collectives, on_device(): return lax.psum(linear + 0.5 * quad, 'fac')  20.1 us
    gather x1, local copies, waits for them, and re-layouts, on_device(): loading_rows[outgoing].reshape(owners, per_source, block_rows, factor_draws)  7.45 us
    all_to_all x1, starting transfers between devices, on_device(): lax.all_to_all(outbound, 'fac', split_axis=0, concat_axis=0, tiled=True)  7.41 us
    all_gather x1, blocking collectives, on_device(): lax.all_gather(gamma, 'scn', axis=1, tiled=True)  7.17 us
    dot_general x1, matrix products, on_device(): jnp.einsum('rbk,ks->rbs', picked, draws, preferred_element_type=jnp.float32)  5.62 us
    gather x1, local copies, waits for them, and re-layouts, on_device(): inbound.reshape(owners * per_source, block_rows, factor_draws)[arrival]  5.31 us
    dot_general x1, matrix products, on_device(): jnp.dot(delta[None, :], loadings, preferred_element_type=jnp.float32, pre...  4.55 us
  transfers between devices with their start and end apart: 1, of which 1 were waited for; matrix products, arithmetic and copies ran while one was open for 4% of the time, Pallas kernels for 0%

commit v1 on v0

v1 whole, which is shorter than its diff:
```python
import functools

import jax
import jax.numpy as jnp
from jax import lax
from jax.experimental import pallas as pl
from jax.experimental.pallas import tpu as pltpu
from jax.sharding import PartitionSpec as P

MESH = pl.DeviceIdType.MESH
CHUNKS = 8


def pack(owners, per_source, capacity, part,
         rows_ref, cols_ref, count_ref, load_ref,
         out_ref, own_ref, arrival_ref, weight_ref, index, seen, sems, own_sems):
    me = lax.axis_index("fac")
    mine = lax.axis_index("scn")
    local_blocks = load_ref.shape[0]
    low = me * local_blocks
    strip = pl.ds(pl.multiple_of(mine * part, part), part)

    def one_owner(step, carry):
        owner = lax.rem(me + step, owners)
        base = owner * capacity
        count = jnp.int32(0)
        for request in range(2 * capacity):
            ref = rows_ref if request % 2 == 0 else cols_ref
            offset = ref[base + request // 2] - low
            index[count] = offset
            count = count + ((offset >= 0) & (offset < local_blocks)).astype(jnp.int32)
        for k in range(per_source):
            block = jnp.where(k < count, index[k], 0)

            @pl.when(step > 0)
            def _():
                pltpu.make_async_copy(
                    load_ref.at[block, strip, :], out_ref.at[owner, k], sems.at[step, k]
                ).start()

            @pl.when(step == 0)
            def _():
                pltpu.make_async_copy(load_ref.at[block], own_ref.at[k], own_sems.at[k]).start()

        return carry

    for k in range(per_source + 1):
        index[k] = 0
    lax.fori_loop(1, owners, one_owner, 0)
    one_owner(0, 0)

    for h in range(owners):
        seen[h] = 0
    base = me * capacity
    for request in range(2 * capacity):
        ref = rows_ref if request % 2 == 0 else cols_ref
        source = lax.div(ref[base + request // 2], jnp.int32(local_blocks))
        position = seen[source]
        arrival_ref[request] = source * per_source + position
        seen[source] = position + 1
    live = count_ref[me]
    for slot in range(capacity):
        level = jnp.where(rows_ref[base + slot] == cols_ref[base + slot], 0.5, 1.0)
        weight_ref[slot] = jnp.where(slot < live, level, 0.0).astype(jnp.float32)

    def finish(step, carry):
        for k in range(per_source):
            pltpu.make_async_copy(
                load_ref.at[0, strip, :], out_ref.at[lax.rem(me + step, owners), k], sems.at[step, k]
            ).wait()
        return carry

    lax.fori_loop(1, owners, finish, 0)
    for k in range(per_source):
        pltpu.make_async_copy(load_ref.at[0], own_ref.at[k], own_sems.at[k]).wait()


def three_parts(values):
    first = values.astype(jnp.bfloat16).astype(jnp.float32)
    rest = values - first
    second = rest.astype(jnp.bfloat16).astype(jnp.float32)
    third = rest - second
    shape = (16, values.shape[1])
    row = lax.broadcasted_iota(jnp.int32, shape, 0)
    spread = [jnp.broadcast_to(v, shape) for v in (first, second, third)]
    zero = jnp.zeros(shape, jnp.float32)
    both = jnp.where(row == 0, spread[0], jnp.where(row == 1, spread[1], jnp.where(row == 2, spread[2], zero)))
    return both.astype(jnp.bfloat16)


def main_kernel(owners, groups, per_source, capacity, part,
                arrival_ref, weight_ref, out_q, own_hbm, load_hbm, draws_hbm, delta_ref, gamma_hbm,
                result_ref,
                loads, draws, own, inbound, shocks, gam, fold, linear, sums,
                load_sem, in_sem, main_s, main_r, x_s, x_r, core_s, core_r, sum_s, sum_r):
    me = lax.axis_index("fac")
    mine = lax.axis_index("scn")
    chips = groups // 2
    core = lax.rem(mine, 2)
    chip = lax.div(mine, 2)
    partner = mine + 1 - 2 * core

    def wrap(value, size):
        return lax.rem(value + size, size)

    def group_of(chip_index):
        return chip_index * 2 + core

    def strip(q):
        return pl.ds(pl.multiple_of(q * part, part), part)

    barrier = pltpu.get_barrier_semaphore()
    for d in range(1, owners):
        pl.semaphore_signal(barrier, inc=1, device_id={"fac": wrap(me + d, owners)}, device_id_type=MESH)
    for j in range(1, chips):
        pl.semaphore_signal(barrier, inc=1, device_id={"scn": group_of(wrap(chip + j, chips))}, device_id_type=MESH)
    pl.semaphore_signal(barrier, inc=1, device_id={"scn": partner}, device_id_type=MESH)

    gamma_in = pltpu.make_async_copy(gamma_hbm, gam.at[:, strip(mine), :], in_sem.at[0])
    draws_in = pltpu.make_async_copy(draws_hbm, draws, in_sem.at[1])
    own_in = pltpu.make_async_copy(own_hbm, own, in_sem.at[2])
    gamma_in.start()
    draws_in.start()
    own_in.start()
    rows = loads.shape[1]

    def load_copy(c):
        return pltpu.make_async_copy(
            load_hbm.at[pl.ds(pl.multiple_of(c * rows, rows), rows), :], loads.at[c], load_sem.at[c]
        )

    for c in range(CHUNKS):
        load_copy(c).start()

    pl.semaphore_wait(barrier, owners - 1 + chips)

    def main_copy(d):
        return pltpu.make_async_remote_copy(
            src_ref=out_q.at[wrap(me + d, owners)], dst_ref=inbound.at[me, :, strip(mine), :],
            send_sem=main_s.at[d], recv_sem=main_r.at[d],
            device_id={"fac": wrap(me + d, owners)}, device_id_type=MESH,
        )

    def main_arrival(d):
        return pltpu.make_async_remote_copy(
            src_ref=out_q.at[me], dst_ref=inbound.at[wrap(me - d, owners), :, strip(mine), :],
            send_sem=main_s.at[d], recv_sem=main_r.at[d],
            device_id={"fac": wrap(me + d, owners)}, device_id_type=MESH,
        )

    def start_main(d, carry):
        main_copy(d).start()
        return carry

    lax.fori_loop(1, owners, start_main, 0)

    def place(d, q):
        if d is None:
            return gam.at[:, strip(q), :]
        return inbound.at[wrap(me - d, owners), :, strip(q), :]

    def at(d):
        return 0 if d is None else d

    def x_copy(d, j, q, source=None):
        return pltpu.make_async_remote_copy(
            src_ref=place(d, q) if source is None else source, dst_ref=place(d, q),
            send_sem=x_s.at[at(d), j - 1], recv_sem=x_r.at[at(d), j - 1],
            device_id={"scn": group_of(wrap(chip + j, chips))}, device_id_type=MESH,
        )

    def core_copy(d, j, q, source=None):
        return pltpu.make_async_remote_copy(
            src_ref=place(d, q) if source is None else source, dst_ref=place(d, q),
            send_sem=core_s.at[at(d), j], recv_sem=core_r.at[at(d), j],
            device_id={"scn": partner}, device_id_type=MESH,
        )

    def origin(j):
        return group_of(wrap(chip - j, chips))

    def partners_origin(j):
        return wrap(chip - j, chips) * 2 + 1 - core

    def share(d, source=None):
        for j in range(1, chips):
            x_copy(d, j, mine, source).start()
        core_copy(d, 0, mine, source).start()

    def forward(d):
        for j in range(1, chips):
            x_copy(d, j, origin(j)).wait_recv()
            core_copy(d, j, origin(j)).start()

    def gathered(d):
        for j in range(chips):
            core_copy(d, j, partners_origin(j)).wait_recv()

    def drain(d):
        for j in range(1, chips):
            x_copy(d, j, mine).wait_send()
        core_copy(d, 0, mine).wait_send()
        for j in range(1, chips):
            core_copy(d, j, origin(j)).wait_send()

    share(None, gamma_hbm)
    draws_in.wait()
    own_in.wait()

    def expose(blocks, h):
        flat = blocks.reshape(blocks.shape[0] * blocks.shape[1], blocks.shape[2])
        value = jnp.dot(flat, draws[...], preferred_element_type=jnp.float32).astype(jnp.bfloat16)
        shocks[pl.ds(h * per_source, per_source)] = value.reshape(per_source, blocks.shape[1], value.shape[1])

    expose(own[...], me)
    fold[...] = jnp.zeros_like(fold)

    def step(t, carry):
        @pl.when(t < owners)
        def _():
            main_arrival(t).wait_recv()
            share(t)

        @pl.when(t == 1)
        def _():
            forward(None)

        @pl.when((t > 1) & (t <= owners))
        def _():
            forward(t - 1)

        @pl.when(t <= CHUNKS)
        def _():
            load_copy(t - 1).wait()
            piece = delta_ref[:, pl.ds(pl.multiple_of((t - 1) * rows, rows), rows)]
            fold[...] += jnp.dot(three_parts(piece), loads[t - 1], preferred_element_type=jnp.float32)

        @pl.when(t == owners)
        def _():
            total = jnp.sum(fold[...], axis=0, keepdims=True)
            linear[...] = jnp.dot(three_parts(total), draws[...], preferred_element_type=jnp.float32)

        @pl.when(t > 2)
        def _():
            gathered(t - 2)
            h = wrap(me - (t - 2), owners)
            expose(inbound[h], h)

        return carry

    lax.fori_loop(1, owners + 2, step, 0)
    gamma_in.wait()
    gathered(None)

    columns = draws.shape[1]
    height = gam.shape[1]

    def one_slot(p, total):
        product = jnp.dot(gam[p], shocks[arrival_ref[2 * p + 1]], preferred_element_type=jnp.float32)
        terms = product * shocks[arrival_ref[2 * p]].astype(jnp.float32)
        return total + weight_ref[p] * jnp.sum(terms.reshape(height // 8, 8, columns), axis=0)

    quad = lax.fori_loop(0, capacity, one_slot, jnp.zeros((8, columns), jnp.float32))
    part_sum = jnp.sum(quad, axis=0, keepdims=True) + jnp.sum(linear[...], axis=0, keepdims=True)
    sums[me] = part_sum

    def sum_copy(d):
        return pltpu.make_async_remote_copy(
            src_ref=sums.at[me], dst_ref=sums.at[me],
            send_sem=sum_s.at[d], recv_sem=sum_r.at[d],
            device_id={"fac": wrap(me + d, owners)}, device_id_type=MESH,
        )

    def sum_arrival(d):
        return pltpu.make_async_remote_copy(
            src_ref=sums.at[wrap(me - d, owners)], dst_ref=sums.at[wrap(me - d, owners)],
            send_sem=sum_s.at[d], recv_sem=sum_r.at[d],
            device_id={"fac": wrap(me + d, owners)}, device_id_type=MESH,
        )

    def start_sum(d, carry):
        sum_copy(d).start()
        return carry

    lax.fori_loop(1, owners, start_sum, 0)
    drain(None)

    def drain_step(d, carry):
        main_copy(d).wait_send()
        drain(d)
        return carry

    lax.fori_loop(1, owners, drain_step, 0)

    def wait_sum(d, carry):
        sum_arrival(d).wait_recv()
        return carry

    lax.fori_loop(1, owners, wait_sum, 0)
    result_ref[...] = jnp.sum(sums[...], axis=0)

    def drain_sum(d, carry):
        sum_copy(d).wait_send()
        return carry

    lax.fori_loop(1, owners, drain_sum, 0)


def on_device(loadings, draws, delta, gamma, pair_rows, pair_cols, pair_count):
    owners = lax.axis_size("fac")
    groups = lax.axis_size("scn")
    capacity, part, height = gamma.shape
    local_blocks = loadings.shape[0] // height
    depth, columns = draws.shape
    per_source = 2 * capacity // owners + 1
    chips = groups // 2
    smem = pl.BlockSpec(memory_space=pltpu.SMEM)
    anywhere = pl.BlockSpec(memory_space=pl.ANY)
    vmem = pl.BlockSpec(memory_space=pltpu.VMEM)
    bf16, f32, i32 = jnp.bfloat16, jnp.float32, jnp.int32
    dma = pltpu.SemaphoreType.DMA

    outbound, own, arrival, weight = pl.pallas_call(
        functools.partial(pack, owners, per_source, capacity, part),
        out_shape=(
            jax.ShapeDtypeStruct((owners, per_source, part, depth), bf16),
            jax.ShapeDtypeStruct((per_source, height, depth), bf16),
            jax.ShapeDtypeStruct((2 * capacity,), i32),
            jax.ShapeDtypeStruct((capacity,), f32),
        ),
        in_specs=[smem, smem, smem, anywhere],
        out_specs=(anywhere, anywhere, smem, smem),
        scratch_shapes=[
            pltpu.SMEM((2 * capacity + 1,), i32),
            pltpu.SMEM((owners,), i32),
            dma((owners, per_source)),
            dma((per_source,)),
        ],
        name="pack",
    )(pair_rows, pair_cols, pair_count, loadings.reshape(local_blocks, height, depth))

    rows = loadings.shape[0] // CHUNKS
    result = pl.pallas_call(
        functools.partial(main_kernel, owners, groups, per_source, capacity, part),
        out_shape=jax.ShapeDtypeStruct((1, columns), f32),
        in_specs=[smem, smem, anywhere, anywhere, anywhere, anywhere, vmem, anywhere],
        out_specs=vmem,
        scratch_shapes=[
            pltpu.VMEM((CHUNKS, rows, depth), bf16),
            pltpu.VMEM((depth, columns), bf16),
            pltpu.VMEM((per_source, height, depth), bf16),
            pltpu.VMEM((owners, per_source, height, depth), bf16),
            pltpu.VMEM((owners * per_source, height, columns), bf16),
            pltpu.VMEM((capacity, height, height), bf16),
            pltpu.VMEM((16, depth), f32),
            pltpu.VMEM((16, columns), f32),
            pltpu.VMEM((owners, 1, columns), f32),
            dma((CHUNKS,)),
            dma((3,)),
            dma((owners,)),
            dma((owners,)),
            dma((owners, max(chips - 1, 1))),
            dma((owners, max(chips - 1, 1))),
            dma((owners, chips)),
            dma((owners, chips)),
            dma((owners,)),
            dma((owners,)),
        ],
        compiler_params=pltpu.CompilerParams(
            collective_id=0, has_side_effects=True, vmem_limit_bytes=52 * 2**20
        ),
        name="gather_and_sum",
    )(arrival, weight, outbound, own, loadings, draws, delta.reshape(1, -1), gamma)
    return result.reshape(columns)


def solution(mesh):
    in_specs = (P("fac", None), P(None, "scn"), P("fac"), P("fac", "scn", None), P(), P(), P())
    out_specs = P("scn")
    return jax.shard_map(
        on_device, mesh=mesh, in_specs=in_specs, out_specs=out_specs, check_vma=False
    )
```

time: 166 us -> 122 us (0.73)
  Pallas kernels: 0 us -> 119 us
  waiting for transfers between devices: 102 us -> 0 us
  blocking collectives: 27.2 us -> 0 us
  local copies, waits for them, and re-layouts: 15.5 us -> 2.32 us
  matrix products: 11.6 us -> 0 us
  starting transfers between devices: 7.41 us -> 0 us
    pallas_call x0 -> x2, Pallas kernels: none -> 119 us  [the longest x1 61.5 us: on_device(): pl.pallas_call(functools.partial(main_kernel, owners, groups, per_source,...]
    all_to_all x1 -> x0, waiting for transfers between devices: 102 us -> none  [on_device(): lax.all_to_all(outbound, 'fac', split_axis=0, concat_axis=0, tiled=True)]
    psum x1 -> x0, blocking collectives: 20.1 us -> none  [on_device(): return lax.psum(linear + 0.5 * quad, 'fac')]
    gather x2 -> x0, local copies, waits for them, and re-layouts: 12.8 us -> none  [the longest x1 7.45 us: on_device(): loading_rows[outgoing].reshape(owners, per_source, block_rows, factor_draws)]
    dot_general x4 -> x0, matrix products: 11.6 us -> none  [the longest x1 5.62 us: on_device(): jnp.einsum('rbk,ks->rbs', picked, draws, preferred_element_type=jnp.float32)]
    all_to_all x1 -> x0, starting transfers between devices: 7.41 us -> none  [on_device(): lax.all_to_all(outbound, 'fac', split_axis=0, concat_axis=0, tiled=True)]
    all_gather x1 -> x0, blocking collectives: 7.17 us -> none  [on_device(): lax.all_gather(gamma, 'scn', axis=1, tiled=True)]
    unnamed x8 -> x12, local copies, waits for them, and re-layouts: 0.02 us -> 2.32 us
  transfers between devices with their start and end apart: 1 -> 0, of which waited for: 1 -> 0; matrix products, arithmetic and copies ran while one was open for 4% -> 0% of each run, Pallas kernels for 0% -> 0%
where the time goes in v1:
time: 122 us
  Pallas kernels  119 us (98%)
  local copies, waits for them, and re-layouts  2.32 us (2%)
    pallas_call x1, Pallas kernels, on_device(): pl.pallas_call(functools.partial(main_kernel, owners, groups, per_source,...  61.5 us
    pallas_call x1, Pallas kernels, on_device(): pl.pallas_call(functools.partial(pack, owners, per_source, capacity, part...  57.5 us

profile of v1, /device:TPU:0, one launch (start us, length us, event | category | flops | bytes accessed | tf_op | source)
XLA Modules:
  0.0 122.0 jit_solution(16364260648307282873)
XLA Ops:
  0.0 0.0 copy-start.2
  0.0 0.0 copy-start.3
  0.0 0.0 copy-start
  0.0 57.5 %pack.1 = (bf16[8,5,32,512]{3,2,1,0:T(8,128)(2,1)}, bf16[5,128,512]{2,1,0:T(8,128)(2,1)}, s32[32]{0:T(128)}, f32[16]{0:T(128)}) custom-call(s32[128]{0:T(128)} %rows_ref.1, s32[128]{0:T(128)} %cols_ref.1, s32[8]{0:T(128)} %count_ref.1, bf16[48,128,512]{2,1,0:T(8,128)(2,1)} %bitcast.3), custom_call_target="tpu_custom_call" | custom-call | tf_op jit(solution)/shard_map/pack/pallas_call | solution.py:323
  57.6 0.0 copy-done.2
  57.6 0.0 copy-done.3
  57.6 0.0 copy-done
  57.6 0.0 copy-start.1
  57.6 1.1 copy-done.1
  58.7 0.0 copy-start.4
  58.7 0.7 copy-done.4
  59.3 0.0 copy-start.5
  59.3 0.6 copy-done.5
  59.9 61.5 %gather_and_sum.1 = f32[1,768]{1,0:T(1,128)S(1)} custom-call(s32[32]{0:T(128)S(1)} %copy-done.4, f32[16]{0:T(128)S(1)} %copy-done.5, bf16[8,5,32,512]{3,2,1,0:T(8,128)(2,1)} %get-tuple-element.11.out_q, bf16[5,128,512]{2,1,0:T(8,128)(2,1)S(1)} %copy-done.1, bf16[6144,512]{1,0:T(8,128)(2,1)} %load_hbm.1, bf16[512,768]{1,0:T(8,128)(2,1)S(1)} %copy-done, ...), custom_call_target="tpu_custom_call" | custom-call | tf_op jit(solution)/shard_map/gather_and_sum/pallas_call | solution.py:343
  121.4 0.6 reduce
Async XLA Ops:
  0.0 57.6 %copy-start.2 = (bf16[16,32,128]{2,1,0:T(8,128)(2,1)S(1)}, bf16[16,32,128]{2,1,0:T(8,128)(2,1)}, u32[]{:S(2)}) copy-start(bf16[16,32,128]{2,1,0:T(8,128)(2,1)} %gamma_hbm.1) | copy-start | bytes 393220
  0.0 57.6 %copy-start.3 = (f32[6144]{0:T(1024)S(1)}, f32[6144]{0:T(1024)}, u32[]{:S(2)}) copy-start(f32[6144]{0:T(1024)} %param.9) | copy-start | bytes 73732
  0.0 57.6 %copy-start = (bf16[512,768]{1,0:T(8,128)(2,1)S(1)}, bf16[512,768]{1,0:T(8,128)(2,1)}, u32[]{:S(2)}) copy-start(bf16[512,768]{1,0:T(8,128)(2,1)} %draws_hbm.1) | copy-start | bytes 2359300
  57.6 1.1 copy-start.1
  58.7 0.7 copy-start.4
  59.3 0.6 copy-start.5

commit v2 on v1

--- a/solution.py
+++ b/solution.py
@@ -11,68 +11,43 @@
 CHUNKS = 8
 
 
-def pack(owners, per_source, capacity, part,
-         rows_ref, cols_ref, count_ref, load_ref,
-         out_ref, own_ref, arrival_ref, weight_ref, index, seen, sems, own_sems):
+def tabulate(owners, per_source, local_blocks, wanted_ref, count_ref, table_ref):
     me = lax.axis_index("fac")
-    mine = lax.axis_index("scn")
-    local_blocks = load_ref.shape[0]
-    low = me * local_blocks
-    strip = pl.ds(pl.multiple_of(mine * part, part), part)
-
-    def one_owner(step, carry):
-        owner = lax.rem(me + step, owners)
-        base = owner * capacity
-        count = jnp.int32(0)
-        for request in range(2 * capacity):
-            ref = rows_ref if request % 2 == 0 else cols_ref
-            offset = ref[base + request // 2] - low
-            index[count] = offset
-            count = count + ((offset >= 0) & (offset < local_blocks)).astype(jnp.int32)
-        for k in range(per_source):
-            block = jnp.where(k < count, index[k], 0)
-
-            @pl.when(step > 0)
-            def _():
-                pltpu.make_async_copy(
-                    load_ref.at[block, strip, :], out_ref.at[owner, k], sems.at[step, k]
-                ).start()
-
-            @pl.when(step == 0)
-            def _():
-                pltpu.make_async_copy(load_ref.at[block], own_ref.at[k], own_sems.at[k]).start()
-
-        return carry
-
-    for k in range(per_source + 1):
-        index[k] = 0
-    lax.fori_loop(1, owners, one_owner, 0)
-    one_owner(0, 0)
-
-    for h in range(owners):
-        seen[h] = 0
-    base = me * capacity
-    for request in range(2 * capacity):
-        ref = rows_ref if request % 2 == 0 else cols_ref
-        source = lax.div(ref[base + request // 2], jnp.int32(local_blocks))
-        position = seen[source]
-        arrival_ref[request] = source * per_source + position
-        seen[source] = position + 1
-    live = count_ref[me]
-    for slot in range(capacity):
-        level = jnp.where(rows_ref[base + slot] == cols_ref[base + slot], 0.5, 1.0)
-        weight_ref[slot] = jnp.where(slot < live, level, 0.0).astype(jnp.float32)
-
-    def finish(step, carry):
-        for k in range(per_source):
-            pltpu.make_async_copy(
-                load_ref.at[0, strip, :], out_ref.at[lax.rem(me + step, owners), k], sems.at[step, k]
-            ).wait()
-        return carry
-
-    lax.fori_loop(1, owners, finish, 0)
+    wanted = wanted_ref[...]
+    requests = wanted.shape[1]
+    capacity = requests // 2
+    f32, i32 = jnp.float32, jnp.int32
+    holder = ((wanted.astype(f32) + 0.5) * (1.0 / local_blocks)).astype(i32)
+    square = (requests, requests)
+    earlier = (
+        lax.broadcasted_iota(i32, square, 0) < lax.broadcasted_iota(i32, square, 1)
+    ).astype(f32)
+
+    def rank_of(hit):
+        return jnp.dot(hit.astype(f32), earlier, preferred_element_type=f32).astype(i32)
+
+    hit = holder == me
+    rank = rank_of(hit)
+    offset = wanted - me * local_blocks
+    lane = lax.broadcasted_iota(i32, (owners, 128), 1)
+    picks = jnp.zeros((owners, 128), i32)
     for k in range(per_source):
-        pltpu.make_async_copy(load_ref.at[0], own_ref.at[k], own_sems.at[k]).wait()
+        pick = jnp.sum(jnp.where(hit & (rank == k), offset, 0), axis=1, keepdims=True)
+        picks = picks + jnp.where(lane == k, pick, 0)
+    table_ref[0:owners] = picks
+
+    owner = lax.broadcasted_iota(i32, wanted.shape, 0)
+    is_mine = owner == me
+    my_wanted = jnp.sum(jnp.where(is_mine, wanted, 0), axis=0, keepdims=True)
+    my_holder = jnp.sum(jnp.where(is_mine, holder, 0), axis=0, keepdims=True)
+    from_holder = owner == my_holder
+    position = jnp.sum(jnp.where(from_holder, rank_of(from_holder), 0), axis=0, keepdims=True)
+    arrival = my_holder * per_source + position
+    slot = lax.broadcasted_iota(i32, (1, capacity), 1)
+    level = jnp.where(my_wanted[:, :capacity] == my_wanted[:, capacity:], 1, 2)
+    level = jnp.where(slot < count_ref[me], level, 0)
+    table_ref[owners:owners + 1, 0:requests] = arrival
+    table_ref[owners + 1:owners + 2, 0:capacity] = level
 
 
 def three_parts(values):
@@ -89,9 +64,9 @@
 
 
 def main_kernel(owners, groups, per_source, capacity, part,
-                arrival_ref, weight_ref, out_q, own_hbm, load_hbm, draws_hbm, delta_ref, gamma_hbm,
+                table_ref, load_hbm, draws_hbm, delta_ref, gamma_hbm,
                 result_ref,
-                loads, draws, own, inbound, shocks, gam, fold, linear, sums,
+                loads, draws, strips, out_q, inbound, shocks, gam, fold, linear, sums,
                 load_sem, in_sem, main_s, main_r, x_s, x_r, core_s, core_r, sum_s, sum_r):
     me = lax.axis_index("fac")
     mine = lax.axis_index("scn")
@@ -118,15 +93,17 @@
 
     gamma_in = pltpu.make_async_copy(gamma_hbm, gam.at[:, strip(mine), :], in_sem.at[0])
     draws_in = pltpu.make_async_copy(draws_hbm, draws, in_sem.at[1])
-    own_in = pltpu.make_async_copy(own_hbm, own, in_sem.at[2])
+    strips_in = pltpu.make_async_copy(load_hbm.at[:, strip(mine), :], strips, in_sem.at[2])
+    strips_in.start()
     gamma_in.start()
     draws_in.start()
-    own_in.start()
-    rows = loads.shape[1]
+    local_blocks, height, depth = loads.shape
+    some = local_blocks // CHUNKS
+    rows = some * height
 
     def load_copy(c):
         return pltpu.make_async_copy(
-            load_hbm.at[pl.ds(pl.multiple_of(c * rows, rows), rows), :], loads.at[c], load_sem.at[c]
+            load_hbm.at[pl.ds(c * some, some)], loads.at[pl.ds(c * some, some)], load_sem.at[c]
         )
 
     for c in range(CHUNKS):
@@ -148,7 +125,12 @@
             device_id={"fac": wrap(me + d, owners)}, device_id_type=MESH,
         )
 
+    strips_in.wait()
+
     def start_main(d, carry):
+        owner = wrap(me + d, owners)
+        for k in range(per_source):
+            out_q[owner, k] = strips[table_ref[owner, k]]
         main_copy(d).start()
         return carry
 
@@ -205,14 +187,12 @@
 
     share(None, gamma_hbm)
     draws_in.wait()
-    own_in.wait()
 
     def expose(blocks, h):
         flat = blocks.reshape(blocks.shape[0] * blocks.shape[1], blocks.shape[2])
         value = jnp.dot(flat, draws[...], preferred_element_type=jnp.float32).astype(jnp.bfloat16)
         shocks[pl.ds(h * per_source, per_source)] = value.reshape(per_source, blocks.shape[1], value.shape[1])
 
-    expose(own[...], me)
     fold[...] = jnp.zeros_like(fold)
 
     def step(t, carry):
@@ -229,11 +209,20 @@
         def _():
             forward(t - 1)
 
+        @pl.when(t == 1)
+        def _():
+            for c in range(CHUNKS):
+                load_copy(c).wait()
+
+        @pl.when(t == 2)
+        def _():
+            expose(jnp.stack([loads[table_ref[me, k]] for k in range(per_source)]), me)
+
         @pl.when(t <= CHUNKS)
         def _():
-            load_copy(t - 1).wait()
             piece = delta_ref[:, pl.ds(pl.multiple_of((t - 1) * rows, rows), rows)]
-            fold[...] += jnp.dot(three_parts(piece), loads[t - 1], preferred_element_type=jnp.float32)
+            chunk = loads[pl.ds((t - 1) * some, some)].reshape(rows, depth)
+            fold[...] += jnp.dot(three_parts(piece), chunk, preferred_element_type=jnp.float32)
 
         @pl.when(t == owners)
         def _():
@@ -253,12 +242,11 @@
     gathered(None)
 
     columns = draws.shape[1]
-    height = gam.shape[1]
 
     def one_slot(p, total):
-        product = jnp.dot(gam[p], shocks[arrival_ref[2 * p + 1]], preferred_element_type=jnp.float32)
-        terms = product * shocks[arrival_ref[2 * p]].astype(jnp.float32)
-        return total + weight_ref[p] * jnp.sum(terms.reshape(height // 8, 8, columns), axis=0)
+        product = jnp.dot(gam[p], shocks[table_ref[owners, capacity + p]], preferred_element_type=jnp.float32)
+        terms = product * shocks[table_ref[owners, p]].astype(jnp.float32)
+        return total + (0.5 * table_ref[owners + 1, p].astype(jnp.float32)) * jnp.sum(terms.reshape(height // 8, 8, columns), axis=0)
 
     quad = lax.fori_loop(0, capacity, one_slot, jnp.zeros((8, columns), jnp.float32))
     part_sum = jnp.sum(quad, axis=0, keepdims=True) + jnp.sum(linear[...], axis=0, keepdims=True)
@@ -320,35 +308,27 @@
     bf16, f32, i32 = jnp.bfloat16, jnp.float32, jnp.int32
     dma = pltpu.SemaphoreType.DMA
 
-    outbound, own, arrival, weight = pl.pallas_call(
-        functools.partial(pack, owners, per_source, capacity, part),
-        out_shape=(
-            jax.ShapeDtypeStruct((owners, per_source, part, depth), bf16),
-            jax.ShapeDtypeStruct((per_source, height, depth), bf16),
-            jax.ShapeDtypeStruct((2 * capacity,), i32),
-            jax.ShapeDtypeStruct((capacity,), f32),
-        ),
-        in_specs=[smem, smem, smem, anywhere],
-        out_specs=(anywhere, anywhere, smem, smem),
-        scratch_shapes=[
-            pltpu.SMEM((2 * capacity + 1,), i32),
-            pltpu.SMEM((owners,), i32),
-            dma((owners, per_source)),
-            dma((per_source,)),
-        ],
-        name="pack",
-    )(pair_rows, pair_cols, pair_count, loadings.reshape(local_blocks, height, depth))
-
-    rows = loadings.shape[0] // CHUNKS
+    wanted = jnp.concatenate(
+        [pair_rows.reshape(owners, capacity), pair_cols.reshape(owners, capacity)], axis=1
+    )
+    table = pl.pallas_call(
+        functools.partial(tabulate, owners, per_source, local_blocks),
+        out_shape=jax.ShapeDtypeStruct((owners + 8, 128), i32),
+        in_specs=[vmem, smem],
+        out_specs=vmem,
+        name="tabulate",
+    )(wanted, pair_count)
+
     result = pl.pallas_call(
         functools.partial(main_kernel, owners, groups, per_source, capacity, part),
         out_shape=jax.ShapeDtypeStruct((1, columns), f32),
-        in_specs=[smem, smem, anywhere, anywhere, anywhere, anywhere, vmem, anywhere],
+        in_specs=[smem, anywhere, anywhere, vmem, anywhere],
         out_specs=vmem,
         scratch_shapes=[
-            pltpu.VMEM((CHUNKS, rows, depth), bf16),
+            pltpu.VMEM((local_blocks, height, depth), bf16),
             pltpu.VMEM((depth, columns), bf16),
-            pltpu.VMEM((per_source, height, depth), bf16),
+            pltpu.VMEM((local_blocks, part, depth), bf16),
+            pltpu.VMEM((owners, per_source, part, depth), bf16),
             pltpu.VMEM((owners, per_source, height, depth), bf16),
             pltpu.VMEM((owners * per_source, height, columns), bf16),
             pltpu.VMEM((capacity, height, height), bf16),
@@ -370,7 +350,7 @@
             collective_id=0, has_side_effects=True, vmem_limit_bytes=52 * 2**20
         ),
         name="gather_and_sum",
-    )(arrival, weight, outbound, own, loadings, draws, delta.reshape(1, -1), gamma)
+    )(table, loadings.reshape(local_blocks, height, depth), draws, delta.reshape(1, -1), gamma)
     return result.reshape(columns)
 
 

time: 122 us -> 69.6 us (0.57)
  Pallas kernels: 119 us -> 63 us
  local copies, waits for them, and re-layouts: 2.32 us -> 4.94 us
    pallas_call x1, Pallas kernels: 57.5 us -> 1.61 us  [on_device(): pl.pallas_call(functools.partial(tabulate, owners, per_source, local_bloc...]
    reshape x0 -> x2, local copies, waits for them, and re-layouts: none -> 1.47 us  [the longest x1 0.74 us: on_device(): pair_cols.reshape(owners, capacity)]
    unnamed x12 -> x8, local copies, waits for them, and re-layouts: 2.32 us -> 3.47 us
where the time goes in v2:
time: 69.6 us; the launch traced here: 69.3 us
  Pallas kernels  63 us (91%)
  local copies, waits for them, and re-layouts  4.94 us (7%)
  other arithmetic  1.28 us (2%)
    pallas_call x1, Pallas kernels, on_device(): pl.pallas_call(functools.partial(main_kernel, owners, groups, per_source,...  61.4 us
    unnamed x8, local copies, waits for them, and re-layouts  3.47 us
    pallas_call x1, Pallas kernels, on_device(): pl.pallas_call(functools.partial(tabulate, owners, per_source, local_bloc...  1.61 us

profile of v2, /device:TPU:0, one launch (start us, length us, event | category | flops | bytes accessed | tf_op | source)
XLA Modules:
  0.0 69.3 jit_solution(2645022412355115992)
XLA Ops:
  0.0 0.7 %reshape.15 = s32[8,16]{1,0:T(8,128)S(1)} reshape(s32[128]{0:T(128)} %param.11) | data formatting | bytes 1024 | tf_op jit(solution)/shard_map/reshape | solution.py:312
  0.7 0.7 %reshape.16 = s32[8,16]{1,0:T(8,128)S(1)} reshape(s32[128]{0:T(128)} %param.12) | data formatting | bytes 1024 | tf_op jit(solution)/shard_map/reshape | solution.py:312
  1.5 0.7 pad_add_fusion.wanted_ref
  2.1 1.6 %tabulate.1.table_ref = s32[16,128]{1,0:T(8,128)} custom-call(s32[8,32]{1,0:T(8,128)} %pad_add_fusion.wanted_ref, s32[8]{0:T(128)} %count_ref.1), custom_call_target="tpu_custom_call" | custom-call | tf_op jit(solution)/shard_map/tabulate/pallas_call | solution.py:314
  3.7 0.0 copy-start
  3.7 1.1 %copy-done = bf16[512,768]{1,0:T(8,128)(2,1)S(1)} copy-done((bf16[512,768]{1,0:T(8,128)(2,1)S(1)}, bf16[512,768]{1,0:T(8,128)(2,1)}, u32[]{:S(2)}) %copy-start) | copy-done | bytes 786456
  4.9 0.0 copy-start.1
  4.9 0.9 %copy-done.1 = bf16[16,32,128]{2,1,0:T(8,128)(2,1)S(1)} copy-done((bf16[16,32,128]{2,1,0:T(8,128)(2,1)S(1)}, bf16[16,32,128]{2,1,0:T(8,128)(2,1)}, u32[]{:S(2)}) %copy-start.1) | copy-done | bytes 131096
  5.8 0.0 copy-start.2
  5.8 0.7 %copy-done.2 = s32[16,128]{1,0:T(8,128)S(1)} copy-done((s32[16,128]{1,0:T(8,128)S(1)}, s32[16,128]{1,0:T(8,128)}, u32[]{:S(2)}) %copy-start.2) | copy-done | bytes 8216
  6.5 0.0 copy-start.3
  6.5 0.7 %copy-done.3 = f32[6144]{0:T(1024)S(1)} copy-done((f32[6144]{0:T(1024)S(1)}, f32[6144]{0:T(1024)}, u32[]{:S(2)}) %copy-start.3) | copy-done | bytes 24600
  7.2 61.4 %gather_and_sum.1 = f32[1,768]{1,0:T(1,128)S(1)} custom-call(s32[16,128]{1,0:T(8,128)S(1)} %copy-done.2, bf16[48,128,512]{2,1,0:T(8,128)(2,1)} %bitcast.3, bf16[512,768]{1,0:T(8,128)(2,1)S(1)} %copy-done, f32[1,6144]{1,0:T(1,128)S(1)} %bitcast.2, bf16[16,32,128]{2,1,0:T(8,128)(2,1)S(1)} %copy-done.1), custom_call_target="tpu_custom_call" | custom-call | tf_op jit(solution)/shard_map/gather_and_sum/pallas_call | solution.py:322
  68.7 0.6 reduce
Async XLA Ops:
  3.7 1.1 %copy-start = (bf16[512,768]{1,0:T(8,128)(2,1)S(1)}, bf16[512,768]{1,0:T(8,128)(2,1)}, u32[]{:S(2)}) copy-start(bf16[512,768]{1,0:T(8,128)(2,1)} %draws_hbm.1) | copy-start | bytes 2359300
  4.9 0.9 %copy-start.1 = (bf16[16,32,128]{2,1,0:T(8,128)(2,1)S(1)}, bf16[16,32,128]{2,1,0:T(8,128)(2,1)}, u32[]{:S(2)}) copy-start(bf16[16,32,128]{2,1,0:T(8,128)(2,1)} %gamma_hbm.1) | copy-start | bytes 393220
  5.8 0.7 %copy-start.2 = (s32[16,128]{1,0:T(8,128)S(1)}, s32[16,128]{1,0:T(8,128)}, u32[]{:S(2)}) copy-start(s32[16,128]{1,0:T(8,128)} %tabulate.1.table_ref) | copy-start | bytes 24580
  6.5 0.7 %copy-start.3 = (f32[6144]{0:T(1024)S(1)}, f32[6144]{0:T(1024)}, u32[]{:S(2)}) copy-start(f32[6144]{0:T(1024)} %param.9) | copy-start | bytes 73732

commit v3 on v2

--- a/solution.py
+++ b/solution.py
@@ -9,6 +9,7 @@
 
 MESH = pl.DeviceIdType.MESH
 CHUNKS = 8
+AHEAD = 2
 
 
 def tabulate(owners, per_source, local_blocks, wanted_ref, count_ref, table_ref):
@@ -78,6 +79,15 @@
     def wrap(value, size):
         return lax.rem(value + size, size)
 
+    def peer(t):
+        half, odd = lax.div(t, 2), lax.rem(t, 2)
+        flips = half + odd * (owners // 2)
+        other, bit = 0, 1
+        while bit < owners:
+            other = other + bit * lax.rem(lax.div(me, bit) + lax.div(flips, bit), 2)
+            bit *= 2
+        return other
+
     def group_of(chip_index):
         return chip_index * 2 + core
 
@@ -113,33 +123,33 @@
 
     def main_copy(d):
         return pltpu.make_async_remote_copy(
-            src_ref=out_q.at[wrap(me + d, owners)], dst_ref=inbound.at[me, :, strip(mine), :],
+            src_ref=out_q.at[peer(d)], dst_ref=inbound.at[me, :, strip(mine), :],
             send_sem=main_s.at[d], recv_sem=main_r.at[d],
-            device_id={"fac": wrap(me + d, owners)}, device_id_type=MESH,
+            device_id={"fac": peer(d)}, device_id_type=MESH,
         )
 
     def main_arrival(d):
         return pltpu.make_async_remote_copy(
-            src_ref=out_q.at[me], dst_ref=inbound.at[wrap(me - d, owners), :, strip(mine), :],
+            src_ref=out_q.at[me], dst_ref=inbound.at[peer(d), :, strip(mine), :],
             send_sem=main_s.at[d], recv_sem=main_r.at[d],
-            device_id={"fac": wrap(me + d, owners)}, device_id_type=MESH,
+            device_id={"fac": peer(d)}, device_id_type=MESH,
         )
 
     strips_in.wait()
 
     def start_main(d, carry):
-        owner = wrap(me + d, owners)
+        owner = peer(d)
         for k in range(per_source):
             out_q[owner, k] = strips[table_ref[owner, k]]
         main_copy(d).start()
         return carry
 
-    lax.fori_loop(1, owners, start_main, 0)
+    lax.fori_loop(1, 1 + min(AHEAD, owners - 1), start_main, 0)
 
     def place(d, q):
         if d is None:
             return gam.at[:, strip(q), :]
-        return inbound.at[wrap(me - d, owners), :, strip(q), :]
+        return inbound.at[peer(d), :, strip(q), :]
 
     def at(d):
         return 0 if d is None else d
@@ -201,6 +211,10 @@
             main_arrival(t).wait_recv()
             share(t)
 
+        @pl.when(t + AHEAD < owners)
+        def _():
+            start_main(t + AHEAD, 0)
+
         @pl.when(t == 1)
         def _():
             forward(None)
@@ -232,7 +246,7 @@
         @pl.when(t > 2)
         def _():
             gathered(t - 2)
-            h = wrap(me - (t - 2), owners)
+            h = peer(t - 2)
             expose(inbound[h], h)
 
         return carry
@@ -248,7 +262,7 @@
         terms = product * shocks[table_ref[owners, p]].astype(jnp.float32)
         return total + (0.5 * table_ref[owners + 1, p].astype(jnp.float32)) * jnp.sum(terms.reshape(height // 8, 8, columns), axis=0)
 
-    quad = lax.fori_loop(0, capacity, one_slot, jnp.zeros((8, columns), jnp.float32))
+    quad = lax.fori_loop(0, capacity, one_slot, jnp.zeros((8, columns), jnp.float32), unroll=4)
     part_sum = jnp.sum(quad, axis=0, keepdims=True) + jnp.sum(linear[...], axis=0, keepdims=True)
     sums[me] = part_sum
 
@@ -256,14 +270,14 @@
         return pltpu.make_async_remote_copy(
             src_ref=sums.at[me], dst_ref=sums.at[me],
             send_sem=sum_s.at[d], recv_sem=sum_r.at[d],
-            device_id={"fac": wrap(me + d, owners)}, device_id_type=MESH,
+            device_id={"fac": peer(d)}, device_id_type=MESH,
         )
 
     def sum_arrival(d):
         return pltpu.make_async_remote_copy(
-            src_ref=sums.at[wrap(me - d, owners)], dst_ref=sums.at[wrap(me - d, owners)],
+            src_ref=sums.at[peer(d)], dst_ref=sums.at[peer(d)],
             send_sem=sum_s.at[d], recv_sem=sum_r.at[d],
-            device_id={"fac": wrap(me + d, owners)}, device_id_type=MESH,
+            device_id={"fac": peer(d)}, device_id_type=MESH,
         )
 
     def start_sum(d, carry):
@@ -347,7 +361,7 @@
             dma((owners,)),
         ],
         compiler_params=pltpu.CompilerParams(
-            collective_id=0, has_side_effects=True, vmem_limit_bytes=52 * 2**20
+            collective_id=0, has_side_effects=True, vmem_limit_bytes=63 * 2**20
         ),
         name="gather_and_sum",
     )(table, loadings.reshape(local_blocks, height, depth), draws, delta.reshape(1, -1), gamma)

time: 69.6 us -> 55.9 us (0.80)
  Pallas kernels: 63 us -> 52.2 us
  local copies, waits for them, and re-layouts: 4.94 us -> 1.47 us
    pallas_call x1, Pallas kernels: 61.4 us -> 50.6 us  [on_device(): pl.pallas_call(functools.partial(main_kernel, owners, groups, per_source,...]
    unnamed x8 -> x0, local copies, waits for them, and re-layouts: 3.47 us -> none
where the time goes in v3:
time: 55.9 us; the launch traced here: 55.6 us
  Pallas kernels  52.2 us (93%)
  other arithmetic  1.95 us (3%)
  local copies, waits for them, and re-layouts  1.47 us (3%)
    pallas_call x1, Pallas kernels, on_device(): pl.pallas_call(functools.partial(main_kernel, owners, groups, per_source,...  50.6 us
    pallas_call x1, Pallas kernels, on_device(): pl.pallas_call(functools.partial(tabulate, owners, per_source, local_bloc...  1.61 us
    pallas_call x1, other arithmetic, on_device(): pl.pallas_call(functools.partial(main_kernel, owners, groups, per_source,...  1.28 us

profile of v3, /device:TPU:0, one launch (start us, length us, event | category | flops | bytes accessed | tf_op | source)
XLA Modules:
  0.0 55.6 jit_solution(13794375433185408474)
XLA Ops:
  0.0 0.7 %reshape.15 = s32[8,16]{1,0:T(8,128)S(1)} reshape(s32[128]{0:T(128)} %param.11) | data formatting | bytes 1024 | tf_op jit(solution)/shard_map/reshape | solution.py:326
  0.7 0.7 %reshape.16 = s32[8,16]{1,0:T(8,128)S(1)} reshape(s32[128]{0:T(128)} %param.12) | data formatting | bytes 1024 | tf_op jit(solution)/shard_map/reshape | solution.py:326
  1.5 0.7 %pad_add_fusion.wanted_ref = s32[8,32]{1,0:T(8,128)} fusion(s32[8,16]{1,0:T(8,128)S(1)} %reshape.16, s32[8,16]{1,0:T(8,128)S(1)} %reshape.15), kind=kLoop, calls=%fused_computation | loop fusion | flops 256 | bytes 2048 | tf_op jit(solution)/shard_map/concatenate | solution.py:325
  2.1 1.6 %tabulate.1.table_ref = s32[16,128]{1,0:T(8,128)} custom-call(s32[8,32]{1,0:T(8,128)} %pad_add_fusion.wanted_ref, s32[8]{0:T(128)} %count_ref.1), custom_call_target="tpu_custom_call" | custom-call | tf_op jit(solution)/shard_map/tabulate/pallas_call | solution.py:328
  3.7 50.6 %gather_and_sum.1 = f32[1,768]{1,0:T(1,128)} custom-call(s32[16,128]{1,0:T(8,128)} %tabulate.1.table_ref, bf16[48,128,512]{2,1,0:T(8,128)(2,1)} %bitcast.2, bf16[512,768]{1,0:T(8,128)(2,1)} %draws_hbm.1, f32[1,6144]{1,0:T(1,128)} %bitcast.3, bf16[16,32,128]{2,1,0:T(8,128)(2,1)} %gamma_hbm.1), custom_call_target="tpu_custom_call" | custom-call | tf_op jit(solution)/shard_map/gather_and_sum/pallas_call | solution.py:336
  54.3 1.3 %reduce = f32[768]{0:T(1024)} reduce(f32[1,768]{1,0:T(1,128)} %gather_and_sum.1, f32[]{:T(128)} %constant), dimensions={0}, to_apply=%pallas_call.7.reduce_sub_computation | reduce | bytes 6148 | tf_op jit(solution)/shard_map/gather_and_sum/pallas_call | solution.py:336
